TPU v7x, 32 devices: a whole 2x2x4 slice. The times are simulated.
32 devices in a mesh: tm: 16 (over z, x, core), mp: 2 (over y).
Axes of the slice: x: 2, y: 2, z: 4, core: 2. Of those that a mesh axis runs over, the one named last changes fastest.
Arguments:
- tokens: bfloat16 [4096, 1024], P('tm'), may hold values from -9 to 9
- norm1_gain: float32 [1024], replicated, may hold values from 0.5 to 1.5
- query_weight: bfloat16 [1024, 1024], P(None, 'mp'), may hold values from -1 to 1
- key_weight: bfloat16 [1024, 1024], P(None, 'mp'), may hold values from -1 to 1
- value_weight: bfloat16 [1024, 1024], P(None, 'mp'), may hold values from -0.1875 to 0.1875
- output_weight: bfloat16 [1024, 1024], P('mp'), may hold values from -5 to 5
- pattern: int32 [32, 8], replicated, may hold values from -1 to 31, as said below
- adjacency: int32 [128, 128], replicated, may hold values 0 or 1
- decay_rate: float32 [1024], P('mp'), may hold values from 0.015625 to 0.1
- norm2_gain: float32 [1024], replicated, may hold values from 0.5 to 1.5
- up_weight: bfloat16 [1024, 4096], P(None, 'mp'), may hold values from -0.1875 to 0.1875
- down_weight: bfloat16 [4096, 1024], P('mp'), may hold values from -0.09375 to 0.09375
Outputs:
- layer_out: bfloat16 [4096, 1024], P('tm', 'mp')
Inputs may be any that keep to these rules, and one draw needn't show every extreme that they name: pattern[b, 0] = b and pattern[b, 1] = b - 1. For the rows of the blocks g * 2 to g * 2 + 1, entry 2 + k (k from 0 to 5) is the same in all these rows: -1 where g < 2^k, else one of the blocks (g - 2^k) * 2 to (g - 2^k) * 2 + 1, never the block g * 2 - 1.
All inputs are finite; a program needn't handle non-finite values.
Results may differ from a plain program's by a relative error of at most 0.01.
Values may be sent and summed in bfloat16 or wider, within the bound.
A program may use at most 64 MiB of HBM per device.

v0:
```python
import math
import jax
import jax.numpy as jnp
from jax import lax
from jax.sharding import PartitionSpec as P

HD = 128


def from_behind(value, axis, steps):
    count = lax.axis_size(axis)
    first, last = (max(0, -steps), min(count, count - steps))
    return lax.ppermute(value, axis, [(source, source + steps) for source in range(first, last)])


def rms_norm(rows, gain):
    widened = rows.astype(jnp.float32)
    square = jnp.mean(widened * widened, axis=-1, keepdims=True)
    return (widened * lax.rsqrt(square + 1e-05) * gain).astype(jnp.bfloat16)


def block_partial(queries, key_rows, value_rows, heads):
    head_size = queries.shape[-1] // heads
    query_split = queries.reshape(queries.shape[:-1] + (heads, head_size))
    key_split = key_rows.reshape(key_rows.shape[:-1] + (heads, head_size))
    value_split = value_rows.reshape(value_rows.shape[:-1] + (heads, head_size))
    scores = jnp.einsum(
        "...qhd,...khd->...hqk", query_split, key_split, preferred_element_type=jnp.float32
    ) * (1.0 / math.sqrt(head_size))
    tops = jnp.max(scores, axis=-1)
    probs = jnp.exp(scores - tops[..., None])
    totals = jnp.sum(probs, axis=-1)
    weights = probs.astype(jnp.bfloat16)
    outputs = jnp.einsum(
        "...hqk,...khd->...qhd", weights, value_split, preferred_element_type=jnp.float32
    )
    return (tops, totals, outputs.reshape(outputs.shape[:-2] + (heads * head_size,)))


def merge_partials(tops, totals, outputs, valid, heads):
    flags = valid[..., None, None]
    masked = jnp.where(flags, tops, -jnp.inf)
    largest = jnp.max(masked, axis=-3)
    factor = jnp.where(flags, jnp.exp(jnp.where(flags, tops, 0.0) - largest[..., None, :, :]), 0.0)
    denom = jnp.sum(factor * totals, axis=-3)
    split = outputs.reshape(outputs.shape[:-1] + (heads, -1))
    numer = jnp.sum(jnp.swapaxes(factor, -1, -2)[..., None] * split, axis=-4)
    result = numer / jnp.swapaxes(denom, -1, -2)[..., None]
    return result.reshape(result.shape[:-2] + (-1,)).astype(jnp.bfloat16)


def running(frames, retain, inject):
    driven = frames.astype(jnp.float32) * inject
    factors = jnp.broadcast_to(retain, driven.shape)

    def join(earlier, later):
        return (earlier[0] * later[0], later[0] * earlier[1] + later[1])

    return lax.associative_scan(join, (factors, driven), axis=0)[1]


def per_device(
    tokens,
    norm1_gain,
    query_weight,
    key_weight,
    value_weight,
    output_weight,
    pattern,
    adjacency,
    decay_rate,
    norm2_gain,
    up_weight,
    down_weight,
):
    groups = lax.axis_size("tm")
    position = lax.axis_index("tm")
    width = query_weight.shape[1]
    heads = width // HD
    sites = adjacency.shape[0]
    steps = tokens.shape[0] // sites
    normed = rms_norm(tokens, norm1_gain)
    queries = (
        jnp.dot(normed, query_weight, preferred_element_type=jnp.float32)
        .astype(jnp.bfloat16)
        .reshape(steps, sites, width)
    )
    key_rows = jnp.dot(normed, key_weight, preferred_element_type=jnp.float32).astype(jnp.bfloat16)
    value_rows = jnp.dot(normed, value_weight, preferred_element_type=jnp.float32).astype(
        jnp.bfloat16
    )
    key_blocks = key_rows.reshape(steps, sites, width)
    value_blocks = value_rows.reshape(steps, sites, width)
    own_entries = lax.dynamic_slice_in_dim(pattern, position * steps, steps, 0)
    remote = own_entries[:, 2:]
    far_count = remote.shape[1]
    key_last, value_last = from_behind((key_blocks[steps - 1], value_blocks[steps - 1]), "tm", 1)
    prior_keys = jnp.concatenate([key_last[None], key_blocks[:-1]], axis=0)
    prior_values = jnp.concatenate([value_last[None], value_blocks[:-1]], axis=0)
    self_part = block_partial(queries, key_blocks, value_blocks, heads)
    prior_part = block_partial(queries, prior_keys, prior_values, heads)
    spread_queries = jnp.broadcast_to(queries[:, None], (steps, far_count, sites, width))
    wanted = pattern[:, 2:].reshape(groups, -1)
    local_pick = wanted - position * steps
    hits = (wanted >= 0) & (local_pick >= 0) & (local_pick < steps)
    selector = jnp.any(
        (local_pick[:, :, None] == jnp.arange(steps, dtype=jnp.int32)[None, None, :])
        & hits[:, :, None],
        axis=1,
    ).astype(jnp.bfloat16)
    send_keys = jnp.einsum(
        "gs,sbf->gbf", selector, key_blocks, preferred_element_type=jnp.float32
    ).astype(jnp.bfloat16)
    send_values = jnp.einsum(
        "gs,sbf->gbf", selector, value_blocks, preferred_element_type=jnp.float32
    ).astype(jnp.bfloat16)
    got_keys, got_values = (
        lax.all_to_all(send_keys, "tm", split_axis=0, concat_axis=0, tiled=True),
        lax.all_to_all(send_values, "tm", split_axis=0, concat_axis=0, tiled=True),
    )
    source = jnp.maximum(remote, 0) // steps
    far_part = block_partial(spread_queries, got_keys[source], got_values[source], heads)
    tops = jnp.concatenate([self_part[0][:, None], prior_part[0][:, None], far_part[0]], axis=1)
    totals = jnp.concatenate([self_part[1][:, None], prior_part[1][:, None], far_part[1]], axis=1)
    outputs = jnp.concatenate([self_part[2][:, None], prior_part[2][:, None], far_part[2]], axis=1)
    block_ids = position * steps + jnp.arange(steps, dtype=jnp.int32)
    valid = jnp.concatenate(
        [jnp.ones((steps, 1), bool), (block_ids > 0)[:, None], remote >= 0], axis=1
    )
    attended = merge_partials(tops, totals, outputs, valid, heads).reshape(steps * sites, width)
    projected = lax.psum_scatter(
        jnp.dot(attended, output_weight, preferred_element_type=jnp.float32),
        "mp",
        scatter_dimension=1,
        tiled=True,
    )
    columns = projected.shape[1]
    own_tokens = lax.dynamic_slice_in_dim(tokens, lax.axis_index("mp") * columns, columns, 1)
    first = (own_tokens.astype(jnp.float32) + projected).astype(jnp.bfloat16)
    links = jnp.maximum(adjacency, jnp.eye(sites, dtype=jnp.int32))
    degree = jnp.sum(links, axis=1).astype(jnp.float32)
    grid = first.reshape(steps, sites, columns)
    mixed = (
        jnp.einsum(
            "st,btc->bsc", links.astype(jnp.bfloat16), grid, preferred_element_type=jnp.float32
        )
        / degree[None, :, None]
    ).astype(jnp.bfloat16)
    retain = jnp.exp(-decay_rate)
    inject = jnp.sqrt(1.0 - retain * retain)
    by_site = lax.all_to_all(mixed, "tm", split_axis=1, concat_axis=0, tiled=True)
    states = running(by_site, retain, inject).astype(jnp.bfloat16)
    smoothed = lax.all_to_all(states, "tm", split_axis=0, concat_axis=1, tiled=True)
    second = (
        first.astype(jnp.float32) + smoothed.reshape(steps * sites, columns).astype(jnp.float32)
    ).astype(jnp.bfloat16)
    whole = lax.all_gather(second, "mp", axis=1, tiled=True)
    normed_late = rms_norm(whole, norm2_gain)
    hidden = jax.nn.gelu(
        jnp.dot(normed_late, up_weight, preferred_element_type=jnp.float32), approximate=True
    ).astype(jnp.bfloat16)
    summed = lax.psum_scatter(
        jnp.dot(hidden, down_weight, preferred_element_type=jnp.float32),
        "mp",
        scatter_dimension=1,
        tiled=True,
    )
    return (second.astype(jnp.float32) + summed).astype(jnp.bfloat16)


def solution(mesh):
    placed = (
        P("tm", None),
        P(),
        P(None, "mp"),
        P(None, "mp"),
        P(None, "mp"),
        P("mp", None),
        P(),
        P(),
        P("mp"),
        P(),
        P(None, "mp"),
        P("mp", None),
    )
    return jax.shard_map(
        per_device, mesh=mesh, in_specs=placed, out_specs=P("tm", "mp"), check_vma=False
    )
```

profile of v0, /device:TPU:0, one launch (start us, length us, event | category | flops | bytes accessed | tf_op | source)
XLA Modules:
  0.0 243.4 jit_solution(6739945608081619143)
XLA Ops:
  6.5 1.3 fusion.16
  7.9 0.7 slice_compare_fusion
  8.6 0.7 slice_subtract_fusion
  9.4 0.1 copy.136
  9.6 0.1 fusion.75
  9.7 1.9 convolution_convert_fusion.2
  11.6 0.8 convolution_convert_fusion
  12.4 2.5 %copy.148 = bf16[16,128,512]{2,1,0:T(8,128)(2,1)} copy(bf16[16,128,512]{2,0,1:T(8,128)(2,1)S(1)} %convolution_convert_fusion) | data formatting | bytes 4194304 | tf_op jit(solution)/shard_map/convert_element_type | solution.py:116
  15.0 7.5 %all-to-all-start.1 = ((bf16[16,128,512]{2,1,0:T(8,128)(2,1)}), bf16[16,128,512]{2,1,0:T(8,128)(2,1)S(1)}, u32[]{:S(2)}, u32[]{:S(2)}) async-start(bf16[16,128,512]{2,1,0:T(8,128)(2,1)} %copy.148), calls=%async_computation.1 | async-start | bytes 4194304 | tf_op jit(solution)/shard_map/all_to_all | solution.py:119
  22.5 1.9 convolution_convert_fusion.3
  24.4 0.7 copy-done.2
  25.1 0.8 convolution_convert_fusion.1
  25.9 2.5 %copy.138 = bf16[16,128,512]{2,1,0:T(8,128)(2,1)} copy(bf16[16,128,512]{2,0,1:T(8,128)(2,1)S(1)} %convolution_convert_fusion.1) | data formatting | bytes 4194304 | tf_op jit(solution)/shard_map/convert_element_type | solution.py:113
  28.3 35.2 %all-to-all-done.1 = bf16[16,128,512]{2,1,0:T(8,128)(2,1)S(1)} async-done(((bf16[16,128,512]{2,1,0:T(8,128)(2,1)}), bf16[16,128,512]{2,1,0:T(8,128)(2,1)S(1)}, u32[]{:S(2)}, u32[]{:S(2)}) %all-to-all-start.1) | async-done | bytes 2097184 | tf_op jit(solution)/shard_map/all_to_all | solution.py:119
  63.6 11.3 %all-to-all-start = ((bf16[16,128,512]{2,1,0:T(8,128)(2,1)}), bf16[16,128,512]{2,1,0:T(8,128)(2,1)}, u32[]{:S(2)}, u32[]{:S(2)}) async-start(bf16[16,128,512]{2,1,0:T(8,128)(2,1)} %copy.138), calls=%async_computation | async-start | bytes 4194304 | tf_op jit(solution)/shard_map/all_to_all | solution.py:118
  74.9 1.7 fusion.94
  76.6 2.9 %collective-permute-start = (bf16[128,512]{1,0:T(8,128)(2,1)}, bf16[128,512]{1,0:T(8,128)(2,1)}, u32[]{:S(2)}, u32[]{:S(2)}) collective-permute-start(bf16[128,512]{1,0:T(8,128)(2,1)} %get-tuple-element.7), channel_id=1, source_target_pairs={{0,2},{2,4},{4,6},{6,8},{8,10},{10,12},{12,14},{14,16},{16,18},{18... | collective-permute-start | bytes 393224 | tf_op jit(solution)/shard_map/ppermute | solution.py:13
  79.5 0.7 fusion.93
  80.2 3.5 %collective-permute-start.1 = (bf16[128,512]{1,0:T(8,128)(2,1)}, bf16[128,512]{1,0:T(8,128)(2,1)}, u32[]{:S(2)}, u32[]{:S(2)}) collective-permute-start(bf16[128,512]{1,0:T(8,128)(2,1)} %get-tuple-element.5), channel_id=1, source_target_pairs={{0,2},{2,4},{4,6},{6,8},{8,10},{10,12},{12,14},{14,16},{16,18},{18... | collective-permute-start | bytes 393224 | tf_op jit(solution)/shard_map/ppermute | solution.py:13
  83.8 1.7 reshape_reshape.11
  85.5 0.8 reshape_reshape.12
  86.5 2.6 %convolution_convert_fusion.4 = bf16[256,512]{1,0:T(8,128)(2,1)} fusion(bf16[1024,512]{1,0:T(8,128)(2,1)} %param.14, bf16[256,1024]{1,0:T(8,128)(2,1)} %param.12, f32[1024]{0:T(1024)S(1)} %copy-done.11, f32[256]{0:T(256)S(1)} %add_rsqrt_fusion.1), kind=kOutput, calls=%fused_computation.34 | convolution fusion | flops 269615104 | bytes 1840128 | tf_op jit(solution)/shard_map/dot_general | solution.py:84
  89.1 1.0 reshape_reshape.10
  90.1 0.7 copy.129
  90.8 0.9 concatenate.47
  91.8 0.7 copy.132
  92.4 1.0 copy.165
  93.6 0.6 copy.128
  94.2 1.3 fusion.97
  95.4 2.0 convolution_bitcast_fusion.2
  97.6 1.6 concatenate.46
  99.2 1.6 copy.131
  100.7 1.7 copy.164
  102.4 1.3 fusion.96
  103.8 2.0 convolution_bitcast_fusion.1
  105.7 1.9 gather_fusion.1
  107.6 2.6 %copy.149 = bf16[12,128,512]{1,2,0:T(8,128)(2,1)} copy(bf16[12,128,512]{2,1,0:T(8,128)(2,1)} %gather_fusion.1) | data formatting | bytes 3145728 | tf_op jit(solution)/shard_map/gather | solution.py:122
  110.2 5.8 %all-to-all-done = bf16[16,128,512]{2,1,0:T(8,128)(2,1)} async-done(((bf16[16,128,512]{2,1,0:T(8,128)(2,1)}), bf16[16,128,512]{2,1,0:T(8,128)(2,1)}, u32[]{:S(2)}, u32[]{:S(2)}) %all-to-all-start) | async-done | bytes 2097184 | tf_op jit(solution)/shard_map/all_to_all | solution.py:118
  116.0 3.4 %gather_fusion = bf16[12,128,512]{2,1,0:T(8,128)(2,1)} fusion(bf16[16,128,512]{2,1,0:T(8,128)(2,1)} %all-to-all-done, s32[1024]{0:T(1024)S(1)} %pad_clamp_fusion), kind=kCustom, calls=%fused_computation | custom fusion | bytes 3145776 | tf_op jit(solution)/shard_map/gather | solution.py:122
  119.4 1.9 copy.140
  121.4 1.3 multiply_reduce_fusion
  122.7 0.7 fusion.1
  123.4 0.7 copy-done.1
  124.1 0.7 convolution_bitcast_fusion
  125.0 0.1 copy-done.3
  125.1 0.2 copy-done.4
  125.3 0.5 fusion
  125.9 0.2 copy.153
  126.1 1.4 fusion.47
  127.6 0.1 fusion.64
  127.7 40.5 %reduce-scatter.3.cloned.1.call-done = f32[256,512]{1,0:T(8,128)} async-done(((f32[256,1024]{1,0:T(8,128)}), f32[256,512]{1,0:T(8,128)}) %reduce-scatter.3.cloned.1.call-update) | async-done | bytes 524304 | tf_op jit(solution)/shard_map/reduce_scatter | solution.py:131
  168.2 1.1 add_convert_fusion.2
  169.3 0.3 fusion.15
  169.6 0.9 copy.155
  170.5 5.6 %all-to-all-start.2 = ((bf16[2,128,512]{2,0,1:T(2,128)(2,1)}), bf16[2,128,512]{2,0,1:T(2,128)(2,1)S(1)}, u32[]{:S(2)}, u32[]{:S(2)}) async-start(bf16[2,128,512]{2,0,1:T(2,128)(2,1)} %copy.155), calls=%async_computation.3 | async-start | bytes 524288 | tf_op jit(solution)/shard_map/all_to_all | solution.py:151
  176.1 10.0 %all-to-all-done.2 = bf16[2,128,512]{2,0,1:T(2,128)(2,1)S(1)} async-done(((bf16[2,128,512]{2,0,1:T(2,128)(2,1)}), bf16[2,128,512]{2,0,1:T(2,128)(2,1)S(1)}, u32[]{:S(2)}, u32[]{:S(2)}) %all-to-all-start.2) | async-done | bytes 262176 | tf_op jit(solution)/shard_map/all_to_all | solution.py:151
  187.1 0.1 pad.39
  187.2 0.1 pad.40
  187.5 12.8 %all_to_all.28 = bf16[32,8,512]{2,1,0:T(8,128)(2,1)S(1)} all-to-all(bf16[32,8,512]{2,1,0:T(8,128)(2,1)S(1)} %add_convert_fusion.1), channel_id=1, replica_groups=mesh['tm'=16,'mp'=2] {'tm'}, dimensions={0} | all-to-all | bytes 524288 | tf_op jit(solution)/shard_map/all_to_all | solution.py:153
  200.5 8.7 %all_gather.3 = bf16[256,1024]{1,0:T(8,128)(2,1)S(1)} all-gather(bf16[256,512]{1,0:T(8,128)(2,1)S(1)} %fusion.36), channel_id=1, replica_groups=mesh['tm'=16,'mp'=2] {'mp'}, dimensions={1}, use_global_device_ids=true | all-gather | bytes 786432 | tf_op jit(solution)/shard_map/all_gather | solution.py:157
  209.3 0.2 fusion.19
  209.5 7.1 %fusion.22 = f32[256,1024]{1,0:T(8,128)} fusion(bf16[2048,1024]{1,0:T(8,128)(2,1)} %param.23, bf16[1024,2048]{1,0:T(8,128)(2,1)} %param.22, bf16[256,1024]{1,0:T(8,128)(2,1)S(1)} %all_gather.3, f32[1024]{0:T(1024)S(1)} %copy-done.12, f32[256]{0:T(256)S(1)} %add_rsqrt_fusion), kind=kOutput, calls=%fused_computation.42 | convolution fusion | flops 2153250816 | bytes 9966592 | tf_op jit(solution)/shard_map/dot_general | solution.py:163
  216.6 18.1 %reduce-scatter.5.cloned.1.call-done = f32[256,512]{1,0:T(8,128)} async-done(((f32[256,1024]{1,0:T(8,128)}), f32[256,512]{1,0:T(8,128)}) %reduce-scatter.5.cloned.1.call-update) | async-done | bytes 524304 | tf_op jit(solution)/shard_map/reduce_scatter | solution.py:162
  234.8 1.8 add_convert_fusion
  (83 shorter events, 2.3 us)
Async XLA Ops:
  6.5 119.5 %copy-start = (bf16[512,1024]{1,0:T(8,128)(2,1)S(1)}, bf16[512,1024]{1,0:T(8,128)(2,1)}, u32[]{:S(2)}) copy-start(bf16[512,1024]{1,0:T(8,128)(2,1)} %param.17) | copy-start | bytes 3145732
  15.0 7.5 %copy-start.11 = (f32[1024]{0:T(1024)S(1)}, f32[1024]{0:T(1024)}, u32[]{:S(2)}) copy-start(f32[1024]{0:T(1024)} %param.13) | copy-start | bytes 12292
  15.0 48.6 %all-to-all-start.1 = ((bf16[16,128,512]{2,1,0:T(8,128)(2,1)}), bf16[16,128,512]{2,1,0:T(8,128)(2,1)S(1)}, u32[]{:S(2)}, u32[]{:S(2)}) async-start(bf16[16,128,512]{2,1,0:T(8,128)(2,1)} %copy.148), calls=%async_computation.1 | async-start | bytes 4194304 | tf_op jit(solution)/shard_map/all_to_all | solution.py:119
  24.4 0.7 copy-start.2
  63.6 52.4 %all-to-all-start = ((bf16[16,128,512]{2,1,0:T(8,128)(2,1)}), bf16[16,128,512]{2,1,0:T(8,128)(2,1)}, u32[]{:S(2)}, u32[]{:S(2)}) async-start(bf16[16,128,512]{2,1,0:T(8,128)(2,1)} %copy.138), calls=%async_computation | async-start | bytes 4194304 | tf_op jit(solution)/shard_map/all_to_all | solution.py:118
  74.8 11.4 %copy-start.8 = (s32[32,8]{0,1:T(8,128)S(1)}, s32[32,8]{0,1:T(8,128)}, u32[]{:S(2)}) copy-start(s32[32,8]{0,1:T(8,128)} %param.18) | copy-start | bytes 3076
  74.9 93.3 %reduce-scatter.3.cloned.1.call-start = ((), (), s32[]{:S(2)}) async-start(), calls=%async_computation.6 | async-start | bytes 1572864 | tf_op jit(solution)/shard_map/reduce_scatter | solution.py:131
  76.6 21.0 %collective-permute-start = (bf16[128,512]{1,0:T(8,128)(2,1)}, bf16[128,512]{1,0:T(8,128)(2,1)}, u32[]{:S(2)}, u32[]{:S(2)}) collective-permute-start(bf16[128,512]{1,0:T(8,128)(2,1)} %get-tuple-element.7), channel_id=1, source_target_pairs={{0,2},{2,4},{4,6},{6,8},{8,10},{10,12},{12,14},{14,16},{16,18},{18... | collective-permute-start | bytes 393224 | tf_op jit(solution)/shard_map/ppermute | solution.py:13
  80.2 20.5 %collective-permute-start.1 = (bf16[128,512]{1,0:T(8,128)(2,1)}, bf16[128,512]{1,0:T(8,128)(2,1)}, u32[]{:S(2)}, u32[]{:S(2)}) collective-permute-start(bf16[128,512]{1,0:T(8,128)(2,1)} %get-tuple-element.5), channel_id=1, source_target_pairs={{0,2},{2,4},{4,6},{6,8},{8,10},{10,12},{12,14},{14,16},{16,18},{18... | collective-permute-start | bytes 393224 | tf_op jit(solution)/shard_map/ppermute | solution.py:13
  119.4 2.0 copy-start.6
  122.7 1.4 copy-start.1
  124.1 0.7 copy-start.9
  124.1 1.0 copy-start.3
  124.1 1.2 copy-start.4
  125.8 1.7 copy-start.7
  125.9 42.3 %copy-start.5 = (bf16[256,1024]{1,0:T(8,128)(2,1)S(1)}, bf16[256,1024]{1,0:T(8,128)(2,1)}, u32[]{:S(2)}) copy-start(bf16[256,1024]{1,0:T(8,128)(2,1)} %param.12) | copy-start | bytes 1572868
  127.5 48.6 %copy-start.10 = (f32[512]{0:T(512)S(1)}, f32[512]{0:T(512)}, u32[]{:S(2)}) copy-start(f32[512]{0:T(512)} %param.20) | copy-start | bytes 6148
  170.5 15.7 %all-to-all-start.2 = ((bf16[2,128,512]{2,0,1:T(2,128)(2,1)}), bf16[2,128,512]{2,0,1:T(2,128)(2,1)S(1)}, u32[]{:S(2)}, u32[]{:S(2)}) async-start(bf16[2,128,512]{2,0,1:T(2,128)(2,1)} %copy.155), calls=%async_computation.3 | async-start | bytes 524288 | tf_op jit(solution)/shard_map/all_to_all | solution.py:151
  176.1 58.7 %reduce-scatter.5.cloned.1.call-start = ((), (), s32[]{:S(2)}) async-start(), calls=%async_computation.7 | async-start | bytes 1572864 | tf_op jit(solution)/shard_map/reduce_scatter | solution.py:162
  200.3 9.1 %copy-start.12 = (f32[1024]{0:T(1024)S(1)}, f32[1024]{0:T(1024)}, u32[]{:S(2)}) copy-start(f32[1024]{0:T(1024)} %param.21) | copy-start | bytes 12292
Sparse Core Ops, SparseCore 0:
  127.7 40.4 reduce-scatter.2
  216.7 17.9 reduce-scatter.4
where the time goes:
time: 244 us; the launch traced here: 243 us
  waiting for transfers between devices  110 us (45%)
  local copies, waits for them, and re-layouts  33.6 us (14%)
  starting transfers between devices  30.9 us (13%)
  matrix products  25.2 us (10%)
  blocking collectives  21.6 us (9%)
  between operations  14 us (6%)
  other arithmetic  8.48 us (3%)
    reduce_scatter x1, waiting for transfers between devices, per_device(): lax.psum_scatter(jnp.dot(attended, output_weight, preferred_element_type=...  40.5 us
    all_to_all x1, waiting for transfers between devices, per_device(): lax.all_to_all(send_values, 'tm', split_axis=0, concat_axis=0, tiled=True)  35.2 us
    reduce_scatter x1, waiting for transfers between devices, per_device(): lax.psum_scatter(jnp.dot(hidden, down_weight, preferred_element_type=jnp....  18.1 us
    all_to_all x1, blocking collectives, per_device(): lax.all_to_all(states, 'tm', split_axis=0, concat_axis=1, tiled=True)  12.8 us
    all_to_all x1, starting transfers between devices, per_device(): lax.all_to_all(send_keys, 'tm', split_axis=0, concat_axis=0, tiled=True)  11.3 us
    all_to_all x1, waiting for transfers between devices, per_device(): lax.all_to_all(mixed, 'tm', split_axis=1, concat_axis=0, tiled=True)  9.97 us
    all_gather x1, blocking collectives, per_device(): whole = lax.all_gather(second, 'mp', axis=1, tiled=True)  8.75 us
    all_to_all x1, starting transfers between devices, per_device(): lax.all_to_all(send_values, 'tm', split_axis=0, concat_axis=0, tiled=True)  7.49 us
  transfers between devices with their start and end apart: 7, of which 5 were waited for; matrix products, arithmetic and copies ran while one was open for 14% of the time, Pallas kernels for 0%

commit v1 on v0

--- a/solution.py
+++ b/solution.py
@@ -5,6 +5,13 @@
 from jax.sharding import PartitionSpec as P
 
 HD = 128
+
+
+def _bring_frames(my_data, group_axis):
+    x_now = lax.all_to_all(
+        jnp.stack(jnp.split(my_data, lax.psum(1, group_axis), 1), axis=0), group_axis, 0, 0
+    )
+    return jnp.concatenate(x_now, 0)
 
 
 def from_behind(value, axis, steps):
@@ -148,7 +155,7 @@
     ).astype(jnp.bfloat16)
     retain = jnp.exp(-decay_rate)
     inject = jnp.sqrt(1.0 - retain * retain)
-    by_site = lax.all_to_all(mixed, "tm", split_axis=1, concat_axis=0, tiled=True)
+    by_site = _bring_frames(mixed, "tm")
     states = running(by_site, retain, inject).astype(jnp.bfloat16)
     smoothed = lax.all_to_all(states, "tm", split_axis=0, concat_axis=1, tiled=True)
     second = (

time: 244 us -> 253 us (1.037)
  local copies, waits for them, and re-layouts: 33.6 us -> 42.4 us
    unnamed x26 -> x41, local copies, waits for them, and re-layouts: 1.75 us -> 10.8 us
where the time goes in v1:
time: 253 us; the launch traced here: 252 us
  waiting for transfers between devices  110 us (43%)
  local copies, waits for them, and re-layouts  42.4 us (17%)
  starting transfers between devices  30.9 us (12%)
  matrix products  25.2 us (10%)
  blocking collectives  21.6 us (9%)
  between operations  14 us (6%)
  other arithmetic  8.43 us (3%)
    reduce_scatter x1, waiting for transfers between devices, per_device(): lax.psum_scatter(jnp.dot(attended, output_weight, preferred_element_type=...  40.5 us
    all_to_all x1, waiting for transfers between devices, per_device(): lax.all_to_all(send_values, 'tm', split_axis=0, concat_axis=0, tiled=True)  35.2 us
    reduce_scatter x1, waiting for transfers between devices, per_device(): lax.psum_scatter(jnp.dot(hidden, down_weight, preferred_element_type=jnp....  18.1 us
    all_to_all x1, blocking collectives, per_device(): lax.all_to_all(states, 'tm', split_axis=0, concat_axis=1, tiled=True)  12.8 us
    all_to_all x1, starting transfers between devices, per_device(): lax.all_to_all(send_keys, 'tm', split_axis=0, concat_axis=0, tiled=True)  11.3 us
    unnamed x41, local copies, waits for them, and re-layouts  10.8 us
    all_to_all x1, waiting for transfers between devices, _bring_frames(): lax.all_to_all(jnp.stack(jnp.split(my_data, lax.psum(1, group_axis), 1),...  9.97 us
    all_gather x1, blocking collectives, per_device(): whole = lax.all_gather(second, 'mp', axis=1, tiled=True)  8.75 us
  transfers between devices with their start and end apart: 7, of which 5 were waited for; matrix products, arithmetic and copies ran while one was open for 14% of the time, Pallas kernels for 0%

profile of v1, /device:TPU:0, one launch (start us, length us, event | category | flops | bytes accessed | tf_op | source)
XLA Modules:
  0.0 252.1 jit_solution(14939175065498012190)
XLA Ops:
  6.5 1.3 fusion.16
  7.9 0.7 slice_compare_fusion
  8.6 0.7 slice_subtract_fusion
  9.7 1.9 convolution_convert_fusion.2
  11.6 0.8 convolution_convert_fusion
  12.4 2.5 copy.136
  15.0 7.5 %all-to-all-start.1 = ((bf16[16,128,512]{2,1,0:T(8,128)(2,1)}), bf16[16,128,512]{2,1,0:T(8,128)(2,1)S(1)}, u32[]{:S(2)}, u32[]{:S(2)}) async-start(bf16[16,128,512]{2,1,0:T(8,128)(2,1)} %copy.136), calls=%async_computation.1 | async-start | bytes 4194304 | tf_op jit(solution)/shard_map/all_to_all | solution.py:126
  22.5 1.9 convolution_convert_fusion.3
  24.4 0.7 copy-done.2
  25.1 0.8 convolution_convert_fusion.1
  25.9 2.5 copy.126
  28.3 35.2 %all-to-all-done.1 = bf16[16,128,512]{2,1,0:T(8,128)(2,1)S(1)} async-done(((bf16[16,128,512]{2,1,0:T(8,128)(2,1)}), bf16[16,128,512]{2,1,0:T(8,128)(2,1)S(1)}, u32[]{:S(2)}, u32[]{:S(2)}) %all-to-all-start.1) | async-done | bytes 2097184 | tf_op jit(solution)/shard_map/all_to_all | solution.py:126
  63.6 11.3 %all-to-all-start = ((bf16[16,128,512]{2,1,0:T(8,128)(2,1)}), bf16[16,128,512]{2,1,0:T(8,128)(2,1)}, u32[]{:S(2)}, u32[]{:S(2)}) async-start(bf16[16,128,512]{2,1,0:T(8,128)(2,1)} %copy.126), calls=%async_computation | async-start | bytes 4194304 | tf_op jit(solution)/shard_map/all_to_all | solution.py:125
  74.9 1.7 fusion.94
  76.6 2.9 %collective-permute-start = (bf16[128,512]{1,0:T(8,128)(2,1)}, bf16[128,512]{1,0:T(8,128)(2,1)}, u32[]{:S(2)}, u32[]{:S(2)}) collective-permute-start(bf16[128,512]{1,0:T(8,128)(2,1)} %get-tuple-element.7), channel_id=1, source_target_pairs={{0,2},{2,4},{4,6},{6,8},{8,10},{10,12},{12,14},{14,16},{16,18},{18... | collective-permute-start | bytes 393224 | tf_op jit(solution)/shard_map/ppermute | solution.py:20
  79.5 0.7 fusion.93
  80.2 3.5 %collective-permute-start.1 = (bf16[128,512]{1,0:T(8,128)(2,1)}, bf16[128,512]{1,0:T(8,128)(2,1)}, u32[]{:S(2)}, u32[]{:S(2)}) collective-permute-start(bf16[128,512]{1,0:T(8,128)(2,1)} %get-tuple-element.5), channel_id=1, source_target_pairs={{0,2},{2,4},{4,6},{6,8},{8,10},{10,12},{12,14},{14,16},{16,18},{18... | collective-permute-start | bytes 393224 | tf_op jit(solution)/shard_map/ppermute | solution.py:20
  83.8 1.7 reshape_reshape.11
  85.5 0.8 reshape_reshape.12
  86.5 2.6 %convolution_convert_fusion.4 = bf16[256,512]{1,0:T(8,128)(2,1)} fusion(bf16[1024,512]{1,0:T(8,128)(2,1)} %param.14, bf16[256,1024]{1,0:T(8,128)(2,1)} %param.12, f32[1024]{0:T(1024)S(1)} %copy-done.11, f32[256]{0:T(256)S(1)} %add_rsqrt_fusion.1), kind=kOutput, calls=%fused_computation.34 | convolution fusion | flops 269615104 | bytes 1840128 | tf_op jit(solution)/shard_map/dot_general | solution.py:91
  89.1 1.0 reshape_reshape.10
  90.1 0.7 copy.117
  90.8 0.9 concatenate.47
  91.8 0.7 copy.120
  92.4 1.0 copy.148
  94.2 1.3 fusion.97
  95.4 2.0 convolution_bitcast_fusion.2
  97.6 1.6 concatenate.46
  99.2 1.6 copy.119
  100.7 1.7 copy.147
  102.4 1.3 fusion.96
  103.8 2.0 convolution_bitcast_fusion.1
  105.7 1.9 gather_fusion.1
  107.6 2.6 %copy.137 = bf16[12,128,512]{1,2,0:T(8,128)(2,1)} copy(bf16[12,128,512]{2,1,0:T(8,128)(2,1)} %gather_fusion.1) | data formatting | bytes 3145728 | tf_op jit(solution)/shard_map/gather | solution.py:129
  110.2 5.8 %all-to-all-done = bf16[16,128,512]{2,1,0:T(8,128)(2,1)} async-done(((bf16[16,128,512]{2,1,0:T(8,128)(2,1)}), bf16[16,128,512]{2,1,0:T(8,128)(2,1)}, u32[]{:S(2)}, u32[]{:S(2)}) %all-to-all-start) | async-done | bytes 2097184 | tf_op jit(solution)/shard_map/all_to_all | solution.py:125
  116.0 3.4 %gather_fusion = bf16[12,128,512]{2,1,0:T(8,128)(2,1)} fusion(bf16[16,128,512]{2,1,0:T(8,128)(2,1)} %all-to-all-done, s32[1024]{0:T(1024)S(1)} %pad_clamp_fusion), kind=kCustom, calls=%fused_computation | custom fusion | bytes 3145776 | tf_op jit(solution)/shard_map/gather | solution.py:129
  119.4 1.9 copy.128
  121.4 1.3 multiply_reduce_fusion
  122.7 0.7 fusion.1
  123.4 0.7 copy-done.1
  124.1 0.7 convolution_bitcast_fusion
  126.1 1.4 fusion.47
  127.7 40.5 %reduce-scatter.3.cloned.1.call-done = f32[256,512]{1,0:T(8,128)} async-done(((f32[256,1024]{1,0:T(8,128)}), f32[256,512]{1,0:T(8,128)}) %reduce-scatter.3.cloned.1.call-update) | async-done | bytes 524304 | tf_op jit(solution)/shard_map/reduce_scatter | solution.py:138
  168.2 1.1 add_convert_fusion.2
  169.5 0.6 constant_dynamic-update-slice_fusion.15
  170.1 0.6 constant_dynamic-update-slice_fusion.14
  170.7 0.6 constant_dynamic-update-slice_fusion.13
  171.3 0.6 constant_dynamic-update-slice_fusion.12
  172.6 0.6 constant_dynamic-update-slice_fusion.10
  173.2 0.6 constant_dynamic-update-slice_fusion.9
  173.8 0.6 constant_dynamic-update-slice_fusion.8
  174.4 0.6 constant_dynamic-update-slice_fusion.7
  175.0 0.6 constant_dynamic-update-slice_fusion.6
  175.6 0.6 constant_dynamic-update-slice_fusion.5
  176.2 0.6 constant_dynamic-update-slice_fusion.4
  178.0 0.6 constant_dynamic-update-slice_fusion.1
  178.6 0.6 constant_dynamic-update-slice_fusion
  179.2 5.6 %all-to-all-start.2 = ((bf16[16,2,8,512]{3,2,1,0:T(8,128)(2,1)}), bf16[16,2,8,512]{3,2,1,0:T(8,128)(2,1)S(1)}, u32[]{:S(2)}, u32[]{:S(2)}) async-start(bf16[16,2,8,512]{3,2,1,0:T(8,128)(2,1)} %constant_dynamic-update-slice_fusion), calls=%async_computation.3 | async-start | bytes 524288 | tf_op jit(solution)/shard_map/all_to_all | solution.py:11
  184.9 10.0 %all-to-all-done.2 = bf16[16,2,8,512]{3,2,1,0:T(8,128)(2,1)S(1)} async-done(((bf16[16,2,8,512]{3,2,1,0:T(8,128)(2,1)}), bf16[16,2,8,512]{3,2,1,0:T(8,128)(2,1)S(1)}, u32[]{:S(2)}, u32[]{:S(2)}) %all-to-all-start.2) | async-done | bytes 262176 | tf_op jit(solution)/shard_map/all_to_all | solution.py:11
  196.2 12.8 %all_to_all.24 = bf16[32,8,512]{2,1,0:T(8,128)(2,1)S(1)} all-to-all(bf16[32,8,512]{2,1,0:T(8,128)(2,1)S(1)} %add_convert_fusion.1), channel_id=1, replica_groups=mesh['tm'=16,'mp'=2] {'tm'}, dimensions={0} | all-to-all | bytes 524288 | tf_op jit(solution)/shard_map/all_to_all | solution.py:160
  209.2 8.7 %all_gather.3 = bf16[256,1024]{1,0:T(8,128)(2,1)S(1)} all-gather(bf16[256,512]{1,0:T(8,128)(2,1)S(1)} %fusion.36), channel_id=1, replica_groups=mesh['tm'=16,'mp'=2] {'mp'}, dimensions={1}, use_global_device_ids=true | all-gather | bytes 786432 | tf_op jit(solution)/shard_map/all_gather | solution.py:164
  218.1 7.1 %fusion.22 = f32[256,1024]{1,0:T(8,128)} fusion(bf16[2048,1024]{1,0:T(8,128)(2,1)} %param.23, bf16[1024,2048]{1,0:T(8,128)(2,1)} %param.22, bf16[256,1024]{1,0:T(8,128)(2,1)S(1)} %all_gather.3, f32[1024]{0:T(1024)S(1)} %copy-done.12, f32[256]{0:T(256)S(1)} %add_rsqrt_fusion), kind=kOutput, calls=%fused_computation.42 | convolution fusion | flops 2153250816 | bytes 9966592 | tf_op jit(solution)/shard_map/dot_general | solution.py:170
  225.3 18.1 %reduce-scatter.5.cloned.1.call-done = f32[256,512]{1,0:T(8,128)} async-done(((f32[256,1024]{1,0:T(8,128)}), f32[256,512]{1,0:T(8,128)}) %reduce-scatter.5.cloned.1.call-update) | async-done | bytes 524304 | tf_op jit(solution)/shard_map/reduce_scatter | solution.py:169
  243.4 1.8 add_convert_fusion
  (96 shorter events, 6.6 us)
Async XLA Ops:
  6.5 119.5 %copy-start = (bf16[512,1024]{1,0:T(8,128)(2,1)S(1)}, bf16[512,1024]{1,0:T(8,128)(2,1)}, u32[]{:S(2)}) copy-start(bf16[512,1024]{1,0:T(8,128)(2,1)} %param.17) | copy-start | bytes 3145732
  15.0 7.5 %copy-start.11 = (f32[1024]{0:T(1024)S(1)}, f32[1024]{0:T(1024)}, u32[]{:S(2)}) copy-start(f32[1024]{0:T(1024)} %param.13) | copy-start | bytes 12292
  15.0 48.6 %all-to-all-start.1 = ((bf16[16,128,512]{2,1,0:T(8,128)(2,1)}), bf16[16,128,512]{2,1,0:T(8,128)(2,1)S(1)}, u32[]{:S(2)}, u32[]{:S(2)}) async-start(bf16[16,128,512]{2,1,0:T(8,128)(2,1)} %copy.136), calls=%async_computation.1 | async-start | bytes 4194304 | tf_op jit(solution)/shard_map/all_to_all | solution.py:126
  24.4 0.7 copy-start.2
  63.6 52.4 %all-to-all-start = ((bf16[16,128,512]{2,1,0:T(8,128)(2,1)}), bf16[16,128,512]{2,1,0:T(8,128)(2,1)}, u32[]{:S(2)}, u32[]{:S(2)}) async-start(bf16[16,128,512]{2,1,0:T(8,128)(2,1)} %copy.126), calls=%async_computation | async-start | bytes 4194304 | tf_op jit(solution)/shard_map/all_to_all | solution.py:125
  74.8 11.4 %copy-start.8 = (s32[32,8]{0,1:T(8,128)S(1)}, s32[32,8]{0,1:T(8,128)}, u32[]{:S(2)}) copy-start(s32[32,8]{0,1:T(8,128)} %param.18) | copy-start | bytes 3076
  74.9 93.3 %reduce-scatter.3.cloned.1.call-start = ((), (), s32[]{:S(2)}) async-start(), calls=%async_computation.6 | async-start | bytes 1572864 | tf_op jit(solution)/shard_map/reduce_scatter | solution.py:138
  76.6 21.0 %collective-permute-start = (bf16[128,512]{1,0:T(8,128)(2,1)}, bf16[128,512]{1,0:T(8,128)(2,1)}, u32[]{:S(2)}, u32[]{:S(2)}) collective-permute-start(bf16[128,512]{1,0:T(8,128)(2,1)} %get-tuple-element.7), channel_id=1, source_target_pairs={{0,2},{2,4},{4,6},{6,8},{8,10},{10,12},{12,14},{14,16},{16,18},{18... | collective-permute-start | bytes 393224 | tf_op jit(solution)/shard_map/ppermute | solution.py:20
  80.2 20.5 %collective-permute-start.1 = (bf16[128,512]{1,0:T(8,128)(2,1)}, bf16[128,512]{1,0:T(8,128)(2,1)}, u32[]{:S(2)}, u32[]{:S(2)}) collective-permute-start(bf16[128,512]{1,0:T(8,128)(2,1)} %get-tuple-element.5), channel_id=1, source_target_pairs={{0,2},{2,4},{4,6},{6,8},{8,10},{10,12},{12,14},{14,16},{16,18},{18... | collective-permute-start | bytes 393224 | tf_op jit(solution)/shard_map/ppermute | solution.py:20
  119.4 2.0 copy-start.6
  122.7 1.4 copy-start.1
  124.1 0.7 copy-start.9
  124.1 1.0 copy-start.3
  124.1 1.2 copy-start.4
  125.8 1.7 copy-start.7
  125.9 42.3 %copy-start.5 = (bf16[256,1024]{1,0:T(8,128)(2,1)S(1)}, bf16[256,1024]{1,0:T(8,128)(2,1)}, u32[]{:S(2)}) copy-start(bf16[256,1024]{1,0:T(8,128)(2,1)} %param.12) | copy-start | bytes 1572868
  127.5 57.4 %copy-start.10 = (f32[512]{0:T(512)S(1)}, f32[512]{0:T(512)}, u32[]{:S(2)}) copy-start(f32[512]{0:T(512)} %param.20) | copy-start | bytes 6148
  179.2 15.7 %all-to-all-start.2 = ((bf16[16,2,8,512]{3,2,1,0:T(8,128)(2,1)}), bf16[16,2,8,512]{3,2,1,0:T(8,128)(2,1)S(1)}, u32[]{:S(2)}, u32[]{:S(2)}) async-start(bf16[16,2,8,512]{3,2,1,0:T(8,128)(2,1)} %constant_dynamic-update-slice_fusion), calls=%async_computation.3 | async-start | bytes 524288 | tf_op jit(solution)/shard_map/all_to_all | solution.py:11
  184.8 58.6 %reduce-scatter.5.cloned.1.call-start = ((), (), s32[]{:S(2)}) async-start(), calls=%async_computation.7 | async-start | bytes 1572864 | tf_op jit(solution)/shard_map/reduce_scatter | solution.py:169
  209.0 9.1 %copy-start.12 = (f32[1024]{0:T(1024)S(1)}, f32[1024]{0:T(1024)}, u32[]{:S(2)}) copy-start(f32[1024]{0:T(1024)} %param.21) | copy-start | bytes 12292
Sparse Core Ops, SparseCore 0:
  127.7 40.4 reduce-scatter.2
  225.4 17.9 reduce-scatter.4
